TPU v7x, 256 devices: a whole 4x4x8 slice. The times are simulated.
256 devices in a mesh: row: 2 (over core), blk: 128 (over y, z, x).
Axes of the slice: x: 4, y: 4, z: 8, core: 2. Of those that a mesh axis runs over, the one named last changes fastest.
Arguments:
- state: float32 [2, 5, 4096, 512], P('row', None, 'blk'), may hold values from -6 to 6
- forcing: float32 [2, 5, 4096, 512], P('row', None, 'blk'), may hold values from -6 to 6
- sigma: float32 [2, 4096, 512], P('row', 'blk'), may hold values from 0.05 to 2
- partner: int32 [2, 4096, 1], P('row', 'blk'), may hold values from 0 to 15; in each aligned block of 32 rows (0 to 31, 32 to 63, ..., all dimensions but the last counted through in order) at most 4 rows name the same one
- loop_weight: float32 [2, 1024], P('row'), may hold values from 0.05 to 0.2
- offset: int32 [1], replicated, may hold values from 0 to 1023
Outputs:
- solution: float32 [2, 5, 4096, 512], P('row', None, 'blk')
- loop_correction: float32 [2, 5, 1024], P('row', None, 'blk')
Inputs may be any that keep to these rules, and one draw needn't show every extreme that they name: Among the 32 face cells of one device no partner slot is named more than 4 times.
All inputs are finite; a program needn't handle non-finite values.
Results may differ from a plain program's by a relative error of at most 0.00011.
Values sent between devices are 32-bit elements; how exact they have to be, the bound alone decides.
A program may use at most 64 MiB of HBM per device.

v0:
```python
import jax
import jax.numpy as jnp
from jax import lax
from jax.sharding import PartitionSpec as P

SECTIONS1 = 3
SECTIONS2 = 3
SECTIONS3 = 4


COEFF = 0.8


def padded_2(cells, sides, width):
    for axis, dim in sides:
        count = lax.axis_size(axis)
        head = lax.slice_in_dim(cells, 0, width, axis=dim)
        tail = lax.slice_in_dim(cells, cells.shape[dim] - width, cells.shape[dim], axis=dim)
        cells = jnp.concatenate(
            [
                lax.ppermute(tail, axis, [(i, (i + 1) % count) for i in range(count)]),
                cells,
                lax.ppermute(head, axis, [((i + 1) % count, i) for i in range(count)]),
            ],
            axis=dim,
        )
    return cells


def from_partner(block, axis, distance):
    count = lax.axis_size(axis)
    route = []
    for low in range(count):
        high = low | 1 << distance
        if high != low and high < count:
            route += [(low, high), (high, low)]
    return lax.ppermute(block, axis, route)


def nonlinear(field):
    q = jnp.mean(field * field, axis=0, keepdims=True)
    return 0.5 * field * q / (1.0 + q)


def apply_operator(extended, sigma_in, scale):
    centre = extended[:, 1:-1]
    across = extended[:, 2:] + extended[:, :-2]
    padded = jnp.pad(centre, ((0, 0), (0, 0), (1, 1)))
    along = padded[:, :, 2:] + padded[:, :, :-2]
    return scale * (4.0 * centre - (across + along)) + sigma_in[None] * centre + nonlinear(centre)


def step_size(sigma_in, scale):
    return COEFF / (4.0 * scale + sigma_in + 1.5)


def smooth_section(field, source, sigma_in, scale, count, wanted):
    tau = step_size(sigma_in, scale)[None]
    start = field
    for section in range(count):
        extended = padded_2(field, (("blk", 1),), 1)
        field = start + 1.0 / (count - section) * tau * (
            source - apply_operator(extended, sigma_in, scale)
        )
    if wanted:
        extended = padded_2(field, (("blk", 1),), 1)
        return (field, source - apply_operator(extended, sigma_in, scale))
    return field


def smooth(field, source, sigma_in, scale, count, wanted):
    return smooth_section(field, source, sigma_in, scale, count, wanted)


def evaluate(field, sigma_in, scale):
    extended = padded_2(field, (("blk", 1),), 1)
    return apply_operator(extended, sigma_in, scale)


def coarsen(x):
    rows, cols = (x.shape[-2], x.shape[-1])
    return x.reshape(x.shape[:-2] + (rows // 2, 2, cols // 2, 2)).mean(axis=(-3, -1))


def refine(x):
    return jnp.repeat(jnp.repeat(x, 2, axis=-2), 2, axis=-1)


def body(state, forcing, sigma, partner, loop_weight, offset):
    row_index = lax.axis_index("row")
    f1 = forcing[0]
    s1 = sigma[0]
    u1, r1 = smooth(state[0], f1, s1, 1.0, SECTIONS1, True)
    face = jnp.where(row_index == 0, r1[:, :, -1], r1[:, :, 0])
    loop_cells = loop_weight.shape[1]
    block_count = lax.axis_size("blk")
    loop_cell = (partner[0, :, 0] * block_count + lax.axis_index("blk")) % loop_cells
    lookup = (loop_cell[:, None] == jnp.arange(loop_cells, dtype=jnp.int32)[None, :]).astype(
        jnp.float32
    )
    contrib = jnp.dot(face, lookup, precision=lax.Precision.HIGHEST)
    own_piece = lax.psum_scatter(contrib, "blk", scatter_dimension=1, tiled=True)
    other_piece = from_partner(own_piece, "row", 0)
    own_loop, other_loop = (
        lax.all_gather(own_piece, "blk", axis=1, tiled=True),
        lax.all_gather(other_piece, "blk", axis=1, tiled=True),
    )
    shift = jnp.where(row_index == 0, -offset[0], offset[0])
    rolled = jnp.roll(other_loop, shift, axis=1)
    correction = loop_weight[0][None, :] * (own_loop + rolled)
    face_fix = jnp.dot(correction, lookup.T, precision=lax.Precision.HIGHEST)
    s2 = coarsen(s1)
    s3 = coarsen(s2)
    u2_start = coarsen(u1)
    f2 = evaluate(u2_start, s2, 0.25) + coarsen(r1)
    u2, r2 = smooth(u2_start, f2, s2, 0.25, SECTIONS2, True)
    u3_start = coarsen(u2)
    f3 = evaluate(u3_start, s3, 0.0625) + coarsen(r2)
    u3 = smooth(u3_start, f3, s3, 0.0625, SECTIONS3, False)
    u2 = u2 + refine(u3 - u3_start)
    u2 = smooth(u2, f2, s2, 0.25, SECTIONS2, False)
    u1 = u1 + refine(u2 - u2_start)
    axial = u1.shape[2]
    columns = jnp.arange(axial, dtype=jnp.int32)
    target = jnp.where(row_index == 0, axial - 1, 0)
    column_mask = (columns == target).astype(jnp.float32)
    u1 = u1 + face_fix[:, :, None] * column_mask[None, None, :]
    u1 = smooth(u1, f1, s1, 1.0, SECTIONS1, False)
    segment = loop_cells // block_count
    loop_out = lax.dynamic_slice_in_dim(correction, lax.axis_index("blk") * segment, segment, 1)
    return (u1[None], loop_out[None])


def solution(mesh):
    placed = (
        P("row", None, "blk", None),
        P("row", None, "blk", None),
        P("row", "blk", None),
        P("row", "blk", None),
        P("row", None),
        P(),
    )
    return jax.shard_map(
        body,
        mesh=mesh,
        in_specs=placed,
        out_specs=(P("row", None, "blk", None), P("row", None, "blk")),
        check_vma=False,
    )
```

profile of v0, /device:TPU:0, one launch (start us, length us, event | category | flops | bytes accessed | tf_op | source)
XLA Modules:
  0.0 1750.3 jit_solution(17621509908090963667)
XLA Ops:
  5.7 8.8 collective-permute-start
  16.8 5.5 reshape_squeeze.3
  41.5 7.6 collective-permute-start.2
  53.9 6.5 multiply_reduce_fusion.4
  65.8 7.4 collective-permute-start.4
  77.7 6.4 multiply_reduce_fusion.3
  86.6 8.8 copy.463
  99.3 7.8 collective-permute-start.8
  107.1 10.8 reduce_sum.227
  132.4 688.9 %all-reduce.18 = f32[5,1024]{1,0:T(8,128)S(1)} all-reduce(f32[5,1024]{1,0:T(8,128)S(1)} %fusion.56), channel_id=2, replica_groups=mesh['row'=2,'blk'=128] {'blk'}, use_global_device_ids=true, to_apply=%region_21.22.clone | all-reduce | flops 5120 | bytes 40960
  821.5 8.8 copy.472
  830.2 10.8 reduce_sum.231
  846.8 366.0 %all_gather.6 = f32[5,1024]{0,1:T(8,128)} all-gather(f32[5,8]{0,1:T(8,128)S(1)} %copy.484), channel_id=1, replica_groups=mesh['row'=2,'blk'=128] {'blk'}, dimensions={1}, use_global_device_ids=true | all-gather | bytes 20640 | tf_op jit(solution)/shard_map/all_gather | solution.py:105
  1214.1 360.5 %all_gather.7 = f32[5,1024]{0,1:T(8,128)} all-gather(f32[5,8]{0,1:T(8,128)S(1)} %copy.485), channel_id=1, replica_groups=mesh['row'=2,'blk'=128] {'blk'}, dimensions={1}, use_global_device_ids=true | all-gather | bytes 20640 | tf_op jit(solution)/shard_map/all_gather | solution.py:106
  1581.3 7.6 collective-permute-done.13
  1613.2 6.1 collective-permute-start.18
  1620.6 7.7 collective-permute-done.19
  1632.1 5.5 collective-permute-done.21
  1641.4 5.7 collective-permute-done.23
  1684.4 7.4 collective-permute-start.31
  1705.2 7.8 collective-permute-start.33
  1717.4 5.8 multiply_reduce_fusion
  1728.6 7.8 collective-permute-start.35
  1740.8 6.7 fusion.8
  (253 shorter events, 174.6 us)
Async XLA Ops:
  5.2 25.3 %collective-permute-start.1 = (f32[5,1,512]{2,1,0:T(1,128)S(1)}, f32[5,1,512]{2,1,0:T(1,128)S(1)}, u32[]{:S(2)}, u32[]{:S(2)}) collective-permute-start(f32[5,1,512]{2,1,0:T(1,128)S(1)} %copy.452), channel_id=1, source_target_pairs={{0,1},{1,2},{2,3},{3,4},{4,5},{5,6},{6,7},{7,8},{8,9},{9,10},{10,1... | collective-permute-start | bytes 30728 | tf_op jit(solution)/shard_map/ppermute | solution.py:21
  5.7 23.3 %collective-permute-start = (f32[5,1,512]{2,1,0:T(1,128)S(1)}, f32[5,1,512]{2,1,0:T(1,128)S(1)}, u32[]{:S(2)}, u32[]{:S(2)}) collective-permute-start(f32[5,1,512]{2,1,0:T(1,128)S(1)} %copy.450), channel_id=1, source_target_pairs={{1,0},{2,1},{3,2},{4,3},{5,4},{6,5},{7,6},{8,7},{9,8},{10,9},{11,1... | collective-permute-start | bytes 30728 | tf_op jit(solution)/shard_map/ppermute | solution.py:23
  41.4 11.0 collective-permute-start.3
  41.5 9.4 collective-permute-start.2
  65.8 10.4 collective-permute-start.5
  99.2 27.2 %collective-permute-start.9 = (f32[5,1,512]{2,1,0:T(1,128)S(1)}, f32[5,1,512]{2,1,0:T(1,128)S(1)}, u32[]{:S(2)}, u32[]{:S(2)}) collective-permute-start(f32[5,1,512]{2,1,0:T(1,128)S(1)} %copy.470), channel_id=1, source_target_pairs={{0,1},{1,2},{2,3},{3,4},{4,5},{5,6},{6,7},{7,8},{8,9},{9,10},{10,1... | collective-permute-start | bytes 30728 | tf_op jit(solution)/shard_map/ppermute | solution.py:21
  99.3 25.7 %collective-permute-start.8 = (f32[5,1,512]{2,1,0:T(1,128)S(1)}, f32[5,1,512]{2,1,0:T(1,128)S(1)}, u32[]{:S(2)}, u32[]{:S(2)}) collective-permute-start(f32[5,1,512]{2,1,0:T(1,128)S(1)} %copy.468), channel_id=1, source_target_pairs={{1,0},{2,1},{3,2},{4,3},{5,4},{6,5},{7,6},{8,7},{9,8},{10,9},{11,1... | collective-permute-start | bytes 30728 | tf_op jit(solution)/shard_map/ppermute | solution.py:23
  120.7 722.6 %collective-permute-start.6 = (f32[5,1,256]{2,1,0:T(1,128)}, f32[5,1,256]{2,1,0:T(1,128)S(1)}, u32[]{:S(2)}, u32[]{:S(2)}) collective-permute-start(f32[5,1,256]{2,1,0:T(1,128)} %get-tuple-element.92), channel_id=1, source_target_pairs={{1,0},{2,1},{3,2},{4,3},{5,4},{6,5},{7,6},{8,7},{9,8},{10,9},{11,1... | collective-permute-start | bytes 15368 | tf_op jit(solution)/shard_map/ppermute | solution.py:23
  123.0 720.3 %collective-permute-start.7 = (f32[5,1,256]{2,1,0:T(1,128)}, f32[5,1,256]{2,1,0:T(1,128)S(1)}, u32[]{:S(2)}, u32[]{:S(2)}) collective-permute-start(f32[5,1,256]{2,1,0:T(1,128)} %get-tuple-element.93), channel_id=1, source_target_pairs={{0,1},{1,2},{2,3},{3,4},{4,5},{5,6},{6,7},{7,8},{8,9},{9,10},{10,1... | collective-permute-start | bytes 15368 | tf_op jit(solution)/shard_map/ppermute | solution.py:21
  821.5 392.6 %collective-permute-start.30 = (f32[5,8]{1,0:T(8,128)S(1)}, f32[5,8]{1,0:T(8,128)S(1)}, u32[]{:S(2)}, u32[]{:S(2)}) collective-permute-start(f32[5,8]{1,0:T(8,128)S(1)} %constant_dynamic-slice_fusion), channel_id=1, source_target_pairs={{0,128},{128,0},{1,129},{129,1},{2,130},{130,2},{3,131},{131,3},{4... | collective-permute-start | bytes 488 | tf_op jit(solution)/shard_map/ppermute | solution.py:37
  844.7 732.7 %collective-permute-start.10 = (f32[5,1,256]{2,1,0:T(1,128)S(1)}, f32[5,1,256]{2,1,0:T(1,128)S(1)}, u32[]{:S(2)}, u32[]{:S(2)}) collective-permute-start(f32[5,1,256]{2,1,0:T(1,128)S(1)} %get-tuple-element.88), channel_id=1, source_target_pairs={{1,0},{2,1},{3,2},{4,3},{5,4},{6,5},{7,6},{8,7},{9,8},{10,9},{11,1... | collective-permute-start | bytes 15368 | tf_op jit(solution)/shard_map/ppermute | solution.py:23
  844.8 732.6 %collective-permute-start.11 = (f32[5,1,256]{2,1,0:T(1,128)S(1)}, f32[5,1,256]{2,1,0:T(1,128)S(1)}, u32[]{:S(2)}, u32[]{:S(2)}) collective-permute-start(f32[5,1,256]{2,1,0:T(1,128)S(1)} %get-tuple-element.89), channel_id=1, source_target_pairs={{0,1},{1,2},{2,3},{3,4},{4,5},{5,6},{6,7},{7,8},{8,9},{9,10},{10,1... | collective-permute-start | bytes 15368 | tf_op jit(solution)/shard_map/ppermute | solution.py:21
  1579.7 9.2 collective-permute-start.13
  1591.0 13.0 collective-permute-start.16
  1591.0 13.0 collective-permute-start.17
  1598.5 13.1 collective-permute-start.14
  1637.8 9.3 collective-permute-start.23
  1649.9 9.1 collective-permute-start.25
  1659.3 9.1 collective-permute-start.27
  1684.3 10.4 collective-permute-start.32
  1704.9 11.0 collective-permute-start.34
  1705.2 9.2 collective-permute-start.33
  1728.5 10.8 collective-permute-start.36
  1728.6 9.2 collective-permute-start.35
  (46 other events, 3378.0 us)
where the time goes:
time: 1760 us; the launch traced here: 1750 us
  blocking collectives  1420 us (81%)
  local copies, waits for them, and re-layouts  107 us (6%)
  starting transfers between devices  86.5 us (5%)
  other arithmetic  80.1 us (5%)
  waiting for transfers between devices  57.1 us (3%)
    unnamed x1, blocking collectives  689 us
    all_gather x1, blocking collectives, body(): lax.all_gather(own_piece, 'blk', axis=1, tiled=True)  366 us
    all_gather x1, blocking collectives, body(): lax.all_gather(other_piece, 'blk', axis=1, tiled=True)  360 us
    ppermute x18, starting transfers between devices, padded_2(): lax.ppermute(head, axis, [((i + 1) % count, i) for i in range(count)])  71.2 us
    ppermute x18, waiting for transfers between devices, padded_2(): lax.ppermute(tail, axis, [(i, (i + 1) % count) for i in range(count)])  44.6 us
  transfers between devices with their start and end apart: 37, of which 19 were waited for; matrix products, arithmetic and copies ran while one was open for 5% of the time, Pallas kernels for 0%

commit v1 on v0

v1 whole, which is shorter than its diff:
```python
import jax
import jax.numpy as jnp
from jax import lax
from jax.experimental import pallas as pl
from jax.experimental.pallas import tpu as pltpu
from jax.sharding import PartitionSpec as P

MESH = pl.DeviceIdType.MESH
V = 5
NB = 128
O1, R1 = 16, 64
O2, R2 = 24, 64
O3, R3 = 16, 40
NY, NZ, NX = 4, 8, 4
HIGH = lax.Precision.HIGHEST


def loop(first, tiles, body):
    def step(k, carry):
        body(first + 8 * k)
        return carry

    lax.fori_loop(0, tiles, step, 0)


def lanes(shape=(8, 128)):
    return lax.broadcasted_iota(jnp.int32, shape, 1)


def rows_of(shape=(8, 128)):
    return lax.broadcasted_iota(jnp.int32, shape, 0)


def apply_l(u_ref, s_ref, r, nt, scale):
    lane = lanes()
    first, last = lane == 0, lane == 127
    here = pl.ds(r, 8)
    centre = [[u_ref[v, t, here, :] for t in range(nt)] for v in range(V)]
    out = [[None] * nt for _ in range(V)]
    diag = []
    for t in range(nt):
        q = centre[0][t] * centre[0][t]
        for v in range(1, V):
            q = q + centre[v][t] * centre[v][t]
        q = q * (1.0 / V)
        diag.append((s_ref[t, here, :] + 4.0 * scale) + (0.5 * q) / (1.0 + q))
    for v in range(V):
        ahead = [pltpu.roll(centre[v][t], 127, 1) for t in range(nt)]
        behind = [pltpu.roll(centre[v][t], 1, 1) for t in range(nt)]
        for t in range(nt):
            right = jnp.where(last, ahead[t + 1] if t + 1 < nt else 0.0, ahead[t])
            left = jnp.where(first, behind[t - 1] if t > 0 else 0.0, behind[t])
            near = (right + left) + (
                u_ref[v, t, pl.ds(r - 1, 8), :] + u_ref[v, t, pl.ds(r + 1, 8), :]
            )
            if scale != 1.0:
                near = scale * near
            out[v][t] = diag[t] * centre[v][t] - near
    return centre, out


def section(dst, start, src, f_ref, s_ref, tau_ref, first, tiles, nt, scale, portion, shift=0):
    def body(r):
        here = pl.ds(r, 8)
        _, out = apply_l(src, s_ref, r, nt, scale)
        for t in range(nt):
            tau = tau_ref[t, here, :] * portion
            for v in range(V):
                dst[v, t, pl.ds(r - shift, 8), :] = start[v, t, here, :] + tau * (
                    f_ref[v, t, here, :] - out[v][t]
                )

    loop(first, tiles, body)


def step_size(tau_ref, s_ref, first, tiles, nt, scale):
    def body(r):
        for t in range(nt):
            tau_ref[t, pl.ds(r, 8), :] = 0.8 / (s_ref[t, pl.ds(r, 8), :] + (4.0 * scale + 1.5))

    loop(first, tiles, body)


def halved(a, b, pick):
    lane = lanes()
    mixed = jnp.where(lane % 2 == 0, a + pltpu.roll(a, 127, 1), b + pltpu.roll(b, 1, 1))
    return jnp.take_along_axis(mixed, pick, axis=1)


def pair_pick():
    lane = lanes()
    return jnp.where(lane < 64, 2 * lane, 2 * lane - 127)


def coarsen_rows(get, f, nt, pick):
    pairs = [get(t, pl.ds(f, 8, stride=2)) + get(t, pl.ds(f + 1, 8, stride=2)) for t in range(nt)]
    if nt == 1:
        return [halved(pairs[0], jnp.zeros_like(pairs[0]), pick) * 0.25]
    return [halved(pairs[2 * t], pairs[2 * t + 1], pick) * 0.25 for t in range(nt // 2)]


def kernel(
    state, forcing, sigma, partner, weight, offset, out, loop_out,
    u1a, u1b, u1c, u1d, f1, s1, t1, outb,
    u2a, u2b, u2c, u2d, r2c, f2, s2, t2,
    u3a, u3b, u3c, r3c, f3, s3, t3,
    onehot, wrow, swap, swapped, comb, zrows, table,
    load_sem, a_send, a_recv, b_send, b_recv, g_send, g_recv, out_sem,
):
    row = lax.axis_index("row")
    b = lax.axis_index("blk")
    right, left = lax.rem(b + 1, NB), lax.rem(b + NB - 1, NB)
    y, z, x = b // 32, lax.rem(b // 4, NZ), lax.rem(b, NX)
    me = y * NX + x
    beside = [(row, right), (row, left)]
    z_peers = [(row, y * 32 + lax.rem(z + d, NZ) * 4 + x) for d in range(1, NZ)]
    xy_peers = [
        (row, lax.rem(y + dy, NY) * 32 + z * 4 + lax.rem(x + dx, NX))
        for dy in range(NY)
        for dx in range(NX)
        if dx or dy
    ]
    partners = beside + [(1 - row, b)] + z_peers + xy_peers
    barrier = pltpu.get_barrier_semaphore()
    for device in partners:
        pl.semaphore_signal(barrier, inc=1, device_id=device, device_id_type=MESH)

    loads = []
    for t in range(4):
        cols = pl.ds(t * 128, 128)
        own = pl.ds(O1, 32)
        loads.append((sigma.at[0, :, cols], s1.at[t, own, :]))
        loads.append((state.at[0, :, :, cols], u1a.at[:, t, own, :]))
        loads.append((forcing.at[0, :, :, cols], f1.at[:, t, own, :]))
    loads = [pltpu.make_async_copy(src, dst, load_sem.at[i]) for i, (src, dst) in enumerate(loads)]
    for copy in loads:
        copy.start()

    lane = lanes()
    pick = pair_pick()
    low = lane % 8
    for k in range(4):
        slot = lax.rem(partner[0, pl.ds(8 * k, 8), :], 8)
        onehot[pl.ds(O1 + 8 * k, 8), :] = (slot == low).astype(jnp.float32)
    weights = jnp.zeros((8, 128), jnp.float32)
    for d, block in enumerate((left, b, right)):
        for p in range(8):
            weights = jnp.where((rows_of() == d) & (low == p), weight[0, p * NB + block], weights)
    wrow[...] = weights

    for copy in loads:
        copy.wait()
    for k in range(2):
        r = O2 + 8 * k
        for t, tile in enumerate(coarsen_rows(lambda t, rows: s1[t, rows, :], O1 + 16 * k, 4, pick)):
            s2[t, pl.ds(r, 8), :] = tile
    pl.semaphore_wait(barrier, len(partners))

    def across(ref, lead, sources, targets, send, recv, first):
        copies = []
        for d in range(2):
            src = ref.at[(slice(None),) * lead + (pl.ds(*sources[d]), slice(None))]
            dst = ref.at[(slice(None),) * lead + (pl.ds(*targets[d]), slice(None))]
            copies.append(
                pltpu.make_async_remote_copy(
                    src_ref=src, dst_ref=dst, send_sem=send.at[first + d], recv_sem=recv.at[first + d],
                    device_id=beside[d], device_id_type=MESH,
                )
            )
        for copy in copies:
            copy.start()
        return copies

    def fine(ref, lead, n, first):
        return across(
            ref, lead, ((O1 + 32 - n, n), (O1, n)), ((O1 - n, n), (O1 + 32, n)), a_send, a_recv, first
        )

    wide = ((O2, 16), (O2, 16)), ((O2 - 16, 16), (O2 + 16, 16))
    a_copies = fine(u1a, 2, 6, 0) + fine(f1, 2, 5, 2) + fine(s1, 1, 5, 4)
    a_late = fine(onehot, 0, 4, 6)
    b_early = across(s2, 1, *wide, b_send, b_recv, 0)
    for copy in a_copies:
        copy.wait_recv()

    step_size(t1, s1, O1 - 8, 6, 4, 1.0)
    section(u1b, u1a, u1a, f1, s1, t1, O1 - 8, 6, 4, 1.0, 1.0 / 3.0)
    section(u1c, u1a, u1b, f1, s1, t1, O1 - 4, 5, 4, 1.0, 0.5)
    section(u1b, u1a, u1c, f1, s1, t1, O1 - 4, 5, 4, 1.0, 1.0)

    target = jnp.where(row == 0, 127, 0)
    at_target = jnp.zeros((8, 128), jnp.int32) + target
    variable = (lane - 64 * row) // 8
    inside = lane >= 64 * row
    swap[...] = jnp.zeros((8, 128), jnp.float32)

    def residual(r):
        here = pl.ds(r, 8)
        _, out_l = apply_l(u1b, s1, r, 4, 1.0)
        mixed = jnp.zeros((8, 128), jnp.float32)
        for v in range(V):
            rest = [f1[v, t, here, :] - out_l[v][t] for t in range(4)]
            for t in range(4):
                u1c[v, t, here, :] = rest[t]
            face = jnp.take_along_axis(jnp.where(row == 0, rest[3], rest[0]), at_target, axis=1)
            mixed = jnp.where((variable == v) & inside, face, mixed)
        swap[...] += mixed * onehot[here, :]

    loop(O1, 4, residual)
    total = jnp.sum(swap[...], axis=0, keepdims=True)
    comb[0:1, :] = total
    to_core = pltpu.make_async_remote_copy(
        src_ref=comb.at[0:1, :], dst_ref=swapped.at[0:1, :], send_sem=g_send.at[0], recv_sem=g_recv.at[0],
        device_id=(1 - row, b), device_id_type=MESH,
    )
    to_core.start()

    for k, r in enumerate((-1, 7, 9)):
        for v in range(V):
            tiles = coarsen_rows(lambda t, rows, v=v: u1b[v, t, rows, :], O1 + 2 * r, 4, pick)
            for t in range(2):
                u2a[v, t, pl.ds(O2 + r, 8), :] = tiles[t]
    for r in (0, 8):
        for v in range(V):
            tiles = coarsen_rows(lambda t, rows, v=v: u1c[v, t, rows, :], O1 + 2 * r, 4, pick)
            for t in range(2):
                r2c[v, t, pl.ds(O2 + r, 8), :] = tiles[t]
    b_copies = across(
        u2a, 2, ((O2 - 1, 16), (O2 + 1, 16)), ((O2 - 17, 16), (O2 + 17, 16)), b_send, b_recv, 2
    )
    b_copies += across(r2c, 2, *wide, b_send, b_recv, 4)

    to_core.wait_recv()
    both = comb[0:1, :] + swapped[0:1, :]
    comb[1:2, :] = both
    zrows[pl.ds(z, 1), :] = both
    z_copies = [
        pltpu.make_async_remote_copy(
            src_ref=comb.at[1:2, :], dst_ref=zrows.at[pl.ds(z, 1), :], send_sem=g_send.at[1],
            recv_sem=g_recv.at[1], device_id=device, device_id_type=MESH,
        )
        for device in z_peers
    ]
    for copy in z_copies:
        copy.start()
    z_all = pltpu.make_async_remote_copy(
        src_ref=zrows.at[0 : NZ - 1, :], dst_ref=zrows.at[0 : NZ - 1, :], send_sem=g_send.at[1],
        recv_sem=g_recv.at[1], device_id=z_peers[0], device_id_type=MESH,
    )
    z_all.wait_recv()
    table[me] = zrows[...]
    t_copies = [
        pltpu.make_async_remote_copy(
            src_ref=zrows, dst_ref=table.at[me], send_sem=g_send.at[2],
            recv_sem=g_recv.at[2], device_id=device, device_id_type=MESH,
        )
        for device in xy_peers
    ]
    for copy in t_copies:
        copy.start()
    t_all = pltpu.make_async_remote_copy(
        src_ref=table.at[0 : NX * NY - 1], dst_ref=table.at[0 : NX * NY - 1], send_sem=g_send.at[2],
        recv_sem=g_recv.at[2], device_id=xy_peers[0], device_id_type=MESH,
    )

    for copy in b_early + b_copies:
        copy.wait_recv()
    step_size(t2, s2, O2 - 16, 6, 2, 0.25)
    portion = 1.0 / 3.0

    def middle_first(r):
        here = pl.ds(r, 8)
        centre, out_l = apply_l(u2a, s2, r, 2, 0.25)
        for t in range(2):
            tau = t2[t, here, :] * portion
            for v in range(V):
                rest = r2c[v, t, here, :]
                f2[v, t, here, :] = out_l[v][t] + rest
                u2b[v, t, here, :] = centre[v][t] + tau * rest

    loop(O2 - 16, 6, middle_first)
    section(u2c, u2a, u2b, f2, s2, t2, O2 - 16, 6, 2, 0.25, 0.5)
    section(u2b, u2a, u2c, f2, s2, t2, O2 - 16, 6, 2, 0.25, 1.0)

    def middle_rest(r):
        here = pl.ds(r, 8)
        _, out_l = apply_l(u2b, s2, r, 2, 0.25)
        for t in range(2):
            for v in range(V):
                u2c[v, t, here, :] = f2[v, t, here, :] - out_l[v][t]

    loop(O2 - 12, 5, middle_rest)

    for k in range(3):
        r, f = O3 - 8 + 8 * k, O2 - 16 + 16 * k
        here = pl.ds(r, 8)
        s3[0, here, :] = coarsen_rows(lambda t, rows: s2[t, rows, :], f, 2, pick)[0]
        t3[0, here, :] = 0.8 / (s3[0, here, :] + 1.75)
        for v in range(V):
            u3a[v, 0, here, :] = coarsen_rows(lambda t, rows, v=v: u2b[v, t, rows, :], f, 2, pick)[0]
            r3c[v, 0, here, :] = coarsen_rows(lambda t, rows, v=v: u2c[v, t, rows, :], f, 2, pick)[0]

    def coarse_first(r):
        here = pl.ds(r, 8)
        centre, out_l = apply_l(u3a, s3, r, 1, 0.0625)
        tau = t3[0, here, :] * 0.25
        for v in range(V):
            rest = r3c[v, 0, here, :]
            f3[v, 0, here, :] = out_l[v][0] + rest
            u3b[v, 0, here, :] = centre[v][0] + tau * rest

    loop(O3 - 8, 3, coarse_first)
    section(u3c, u3a, u3b, f3, s3, t3, O3 - 8, 3, 1, 0.0625, 1.0 / 3.0)
    section(u3b, u3a, u3c, f3, s3, t3, O3 - 4, 2, 1, 0.0625, 0.5)
    section(u3c, u3a, u3b, f3, s3, t3, O3 - 4, 2, 1, 0.0625, 1.0)

    spread = [lane // 2, 64 + lane // 2]
    for k in range(2):
        r, f = O3 - 4 + 8 * k, O2 - 8 + 16 * k
        for v in range(V):
            gain = u3c[v, 0, pl.ds(r, 8), :] - u3a[v, 0, pl.ds(r, 8), :]
            for t in range(2):
                more = jnp.take_along_axis(gain, spread[t], axis=1)
                for odd in range(2):
                    rows = pl.ds(f + odd, 8, stride=2)
                    u2d[v, t, rows, :] = u2b[v, t, rows, :] + more

    section(u2b, u2d, u2d, f2, s2, t2, O2 - 4, 3, 2, 0.25, 1.0 / 3.0)
    section(u2c, u2d, u2b, f2, s2, t2, O2 - 4, 3, 2, 0.25, 0.5)
    section(u2b, u2d, u2c, f2, s2, t2, O2 - 4, 3, 2, 0.25, 1.0)

    for r in (-2, 6, 10):
        f = O1 + 2 * r
        for v in range(V):
            for half in range(2):
                here = pl.ds(O2 + r, 8)
                gain = u2b[v, half, here, :] - u2a[v, half, here, :]
                for part in range(2):
                    t = 2 * half + part
                    more = jnp.take_along_axis(gain, spread[part], axis=1)
                    for odd in range(2):
                        rows = pl.ds(f + odd, 8, stride=2)
                        u1d[v, t, rows, :] = u1b[v, t, rows, :] + more

    for copy in a_late:
        copy.wait_recv()
    t_all.wait_recv()

    turn = jnp.where(row == 0, offset[0], 1024 - offset[0])
    index = rows_of()
    cell_own = 8 * b + index
    near_own = lax.rem(b + NB - 1 + index, NB)
    cell_other = (cell_own + turn) & 1023
    near_other = (near_own + turn) & 1023

    def chosen(block):
        block = block & 127
        place = ((block >> 5) * 4 + (block & 3)) * 8 + ((block >> 2) & 7)
        return (place == lane).astype(jnp.float32)

    wanted = jnp.concatenate(
        [chosen(cell_own), chosen(near_own), chosen(cell_other), chosen(near_other)], axis=0
    )
    found = jnp.dot(
        wanted, table[...].reshape(NB, 128), precision=HIGH, preferred_element_type=jnp.float32
    )
    turned = pltpu.roll(found, 64, 1)
    own = jnp.where(row == 0, found[0:16], turned[0:16])
    other = jnp.where(row == 0, turned[16:32], found[16:32])
    valid = lane < 40
    picked = jnp.where(valid & (low == (b // 16)), own[0:8], 0.0) + jnp.where(
        valid & (low == (cell_other >> 7)), other[0:8], 0.0
    )
    summed = (index == lane // 8).astype(jnp.float32)
    cells = lax.dot_general(
        summed, picked, (((1,), (1,)), ((), ())), precision=HIGH, preferred_element_type=jnp.float32
    )
    scale8 = jnp.zeros((8, 8), jnp.float32)
    for k in range(8):
        scale8 = jnp.where(lanes((8, 8)) == k, weight[0, 8 * b + k], scale8)
    loop_out[0] = (cells * scale8)[0:V]

    rotate = (lane & ~7) | ((lane + (near_other >> 7)) & 7)
    corr = jnp.where(
        valid, wrow[...] * (own[8:16] + jnp.take_along_axis(other[8:16], rotate, axis=1)), 0.0
    )
    swap[...] = corr
    first_col = (lane == 0) & (row == 1)
    last_col = (lane == 127) & (row == 0)
    for k in range(5):
        r = O1 - 4 + 8 * k
        here = pl.ds(r, 8)
        near = index + r
        if k == 0:
            table_row = jnp.where(near < O1, swap[0:1, :], swap[1:2, :])
        elif k == 4:
            table_row = jnp.where(near < O1 + 32, swap[1:2, :], swap[2:3, :])
        else:
            table_row = swap[1:2, :]
        terms = onehot[here, :] * table_row
        for hop in (4, 2, 1):
            terms = terms + pltpu.roll(terms, 128 - hop, 1)
        for v in range(V):
            fix = jnp.take_along_axis(terms, jnp.full((8, 128), 8 * v, jnp.int32), axis=1)
            u1d[v, 0, here, :] += jnp.where(first_col, fix, 0.0)
            u1d[v, 3, here, :] += jnp.where(last_col, fix, 0.0)

    section(u1c, u1d, u1d, f1, s1, t1, O1 - 4, 5, 4, 1.0, 1.0 / 3.0)
    section(u1b, u1d, u1c, f1, s1, t1, O1 - 4, 5, 4, 1.0, 0.5)
    section(outb, u1d, u1b, f1, s1, t1, O1, 4, 4, 1.0, 1.0, shift=O1)

    stores = [
        pltpu.make_async_copy(outb.at[:, t], out.at[0, :, :, pl.ds(t * 128, 128)], out_sem.at[t])
        for t in range(4)
    ]
    for copy in stores:
        copy.start()
    for copy in a_copies + a_late + b_early + b_copies + [to_core]:
        copy.wait_send()
    z_all.wait_send()
    t_all.wait_send()
    for copy in stores:
        copy.wait()


def body(state, forcing, sigma, partner, loop_weight, offset):
    f32 = jnp.float32
    fine, middle, coarse = (V, 4, R1, 128), (V, 2, R2, 128), (V, 1, R3, 128)
    buffers = [fine] * 5 + [(4, R1, 128)] * 2 + [(V, 4, 32, 128)]
    buffers += [middle] * 6 + [(2, R2, 128)] * 2
    buffers += [coarse] * 5 + [(1, R3, 128)] * 2
    buffers += [(R1, 128), (8, 128), (8, 128), (8, 128), (8, 128), (NZ, 128), (NX * NY, NZ, 128)]
    any_space = pl.BlockSpec(memory_space=pl.ANY)
    smem = pl.BlockSpec(memory_space=pltpu.SMEM)
    vmem = pl.BlockSpec(memory_space=pltpu.VMEM)
    dma = pltpu.SemaphoreType.DMA
    return pl.pallas_call(
        kernel,
        out_shape=(
            jax.ShapeDtypeStruct((1, V, 32, 512), f32),
            jax.ShapeDtypeStruct((1, V, 8), f32),
        ),
        in_specs=[any_space, any_space, any_space, vmem, smem, smem],
        out_specs=(any_space, vmem),
        scratch_shapes=[pltpu.VMEM(shape, f32) for shape in buffers]
        + [dma((12,)), dma((8,)), dma((8,)), dma((6,)), dma((6,)), dma((3,)), dma((3,)), dma((4,))],
        compiler_params=pltpu.CompilerParams(
            collective_id=0, has_side_effects=True, vmem_limit_bytes=40 * 1024 * 1024
        ),
        name="fas_cycle",
    )(state, forcing, sigma, partner, loop_weight, offset)


def solution(mesh):
    placed = (
        P("row", None, "blk", None),
        P("row", None, "blk", None),
        P("row", "blk", None),
        P("row", "blk", None),
        P("row", None),
        P(),
    )
    return jax.shard_map(
        body,
        mesh=mesh,
        in_specs=placed,
        out_specs=(P("row", None, "blk", None), P("row", None, "blk")),
        check_vma=False,
    )
```

time: 1760 us -> 41.1 us (0.02)
  blocking collectives: 1420 us -> 0 us
  local copies, waits for them, and re-layouts: 107 us -> 4.77 us
  starting transfers between devices: 86.5 us -> 0 us
  other arithmetic: 80.1 us -> 0 us
  waiting for transfers between devices: 57.1 us -> 0 us
  Pallas kernels: 0 us -> 34.3 us
    all_gather x2 -> x0, blocking collectives: 726 us -> none  [the longest x1 366 us: body(): lax.all_gather(own_piece, 'blk', axis=1, tiled=True)]
    unnamed x1 -> x0, blocking collectives: 689 us -> none
    ppermute x37 -> x0, starting transfers between devices: 86.5 us -> none  [the longest x18 71.2 us: padded_2(): lax.ppermute(head, axis, [((i + 1) % count, i) for i in range(count)])]
    reduce_sum x23 -> x0, other arithmetic: 60.9 us -> none  [the longest x6 32.9 us: coarsen(): x.reshape(x.shape[:-2] + (rows // 2, 2, cols // 2, 2)).mean(axis=(-3, -1))]
    ppermute x37 -> x0, waiting for transfers between devices: 57.1 us -> none  [the longest x18 44.6 us: padded_2(): lax.ppermute(tail, axis, [(i, (i + 1) % count) for i in range(count)])]
    pallas_call x0 -> x1, Pallas kernels: none -> 34.3 us  [body(): pl.pallas_call(kernel, out_shape=(jax.ShapeDtypeStruct((1, V, 32, 512), f...]
    slice x32 -> x0, local copies, waits for them, and re-layouts: 32.9 us -> none  [the longest x25 23.5 us: padded_2(): head = lax.slice_in_dim(cells, 0, width, axis=dim)]
    ppermute x15 -> x0, local copies, waits for them, and re-layouts: 21.3 us -> none  [the longest x7 10.6 us: padded_2(): lax.ppermute(tail, axis, [(i, (i + 1) % count) for i in range(count)])]
  transfers between devices with their start and end apart: 37 -> 0, of which waited for: 19 -> 0; matrix products, arithmetic and copies ran while one was open for 5% -> 0% of each run, Pallas kernels for 0% -> 0%
where the time goes in v1:
time: 41.1 us; the launch traced here: 40.4 us
  Pallas kernels  34.3 us (83%)
  local copies, waits for them, and re-layouts  4.77 us (12%)
  between operations  1.33 us (3%)
    pallas_call x1, Pallas kernels, body(): pl.pallas_call(kernel, out_shape=(jax.ShapeDtypeStruct((1, V, 32, 512), f...  34.3 us
    unnamed x12, local copies, waits for them, and re-layouts  4.19 us

profile of v1, /device:TPU:0, one launch (start us, length us, event | category | flops | bytes accessed | tf_op | source)
XLA Modules:
  0.0 40.4 jit_solution(3447593184122152245)
XLA Ops:
  0.6 0.0 copy-start.4
  1.3 0.0 copy-done.4
  1.3 0.0 copy-start.3
  1.3 0.1 copy.8.partner
  1.4 0.6 %copy-done.3 = f32[1,1024]{1,0:T(1,128)S(1)} copy-done((f32[1,1024]{1,0:T(1,128)S(1)}, f32[1,1024]{1,0:T(1,128)}, u32[]{:S(2)}) %copy-start.3) | copy-done | bytes 4120
  2.0 0.0 copy-start
  2.0 1.0 %copy-done = f32[1,5,32,512]{3,2,1,0:T(8,128)S(1)} copy-done((f32[1,5,32,512]{3,2,1,0:T(8,128)S(1)}, f32[1,5,32,512]{3,2,1,0:T(8,128)}, u32[]{:S(2)}) %copy-start) | copy-done | bytes 327704
  3.0 0.0 copy-start.1
  3.0 1.0 %copy-done.1 = f32[1,5,32,512]{3,2,1,0:T(8,128)S(1)} copy-done((f32[1,5,32,512]{3,2,1,0:T(8,128)S(1)}, f32[1,5,32,512]{3,2,1,0:T(8,128)}, u32[]{:S(2)}) %copy-start.1) | copy-done | bytes 327704
  3.9 0.0 copy-start.2
  3.9 0.8 %copy-done.2 = f32[1,32,512]{2,1,0:T(8,128)S(1)} copy-done((f32[1,32,512]{2,1,0:T(8,128)S(1)}, f32[1,32,512]{2,1,0:T(8,128)}, u32[]{:S(2)}) %copy-start.2) | copy-done | bytes 65560
  4.8 34.3 %fas_cycle.1 = (f32[1,5,32,512]{3,2,1,0:T(8,128)S(1)}, f32[1,5,8]{2,1,0:T(8,128)S(1)}) custom-call(f32[1,5,32,512]{3,2,1,0:T(8,128)S(1)} %copy-done, f32[1,5,32,512]{3,2,1,0:T(8,128)S(1)} %copy-done.1, f32[1,32,512]{2,1,0:T(8,128)S(1)} %copy-done.2, s32[1,32,1]{2,1,0:T(8,128)S(1)} %copy.8.partner, f32[1,1024]{1,0:T(1,128)S(1)} %copy-done.3, s32[1]{0:T(128)S(6)} %copy.11.offset), custom_call_target="tpu_custom_call" | custom-call | tf_op jit(solution)/shard_map/fas_cycle/pallas_call | solution.py:437
  39.1 0.6 %copy.9 = f32[1,5,8]{2,0,1:T(1,128)} copy(f32[1,5,8]{2,1,0:T(8,128)S(1)} %get-tuple-element.3) | data formatting | bytes 320 | tf_op jit(solution)/shard_map/fas_cycle/pallas_call | solution.py:437
  39.6 0.7 %copy.12 = f32[1,5,32,512]{3,2,1,0:T(8,128)} copy(f32[1,5,32,512]{3,2,1,0:T(8,128)S(1)} %get-tuple-element.6) | data formatting | bytes 655360
Async XLA Ops:
  0.6 0.7 %copy-start.4 = (s32[1,32,1]{1,2,0:T(1,128)S(1)}, s32[1,32,1]{1,2,0:T(1,128)}, u32[]{:S(2)}) copy-start(s32[1,32,1]{1,2,0:T(1,128)} %param.9) | copy-start | bytes 388
  1.3 0.7 %copy-start.3 = (f32[1,1024]{1,0:T(1,128)S(1)}, f32[1,1024]{1,0:T(1,128)}, u32[]{:S(2)}) copy-start(f32[1,1024]{1,0:T(1,128)} %weight.1) | copy-start | bytes 12292
  2.0 1.0 %copy-start = (f32[1,5,32,512]{3,2,1,0:T(8,128)S(1)}, f32[1,5,32,512]{3,2,1,0:T(8,128)}, u32[]{:S(2)}) copy-start(f32[1,5,32,512]{3,2,1,0:T(8,128)} %state.1) | copy-start | bytes 983044
  3.0 1.0 %copy-start.1 = (f32[1,5,32,512]{3,2,1,0:T(8,128)S(1)}, f32[1,5,32,512]{3,2,1,0:T(8,128)}, u32[]{:S(2)}) copy-start(f32[1,5,32,512]{3,2,1,0:T(8,128)} %forcing.1) | copy-start | bytes 983044
  3.9 0.8 %copy-start.2 = (f32[1,32,512]{2,1,0:T(8,128)S(1)}, f32[1,32,512]{2,1,0:T(8,128)}, u32[]{:S(2)}) copy-start(f32[1,32,512]{2,1,0:T(8,128)} %sigma.1) | copy-start | bytes 196612

commit v2 on v1

--- a/solution.py
+++ b/solution.py
@@ -20,7 +20,7 @@
         body(first + 8 * k)
         return carry
 
-    lax.fori_loop(0, tiles, step, 0)
+    lax.fori_loop(0, tiles, step, 0, unroll=2 if tiles % 2 == 0 else 1)
 
 
 def lanes(shape=(8, 128)):
@@ -100,11 +100,11 @@
 
 
 def kernel(
-    state, forcing, sigma, partner, weight, offset, out, loop_out,
+    state, forcing, sigma, partner_in, weight_in, offset, out, loop_out,
     u1a, u1b, u1c, u1d, f1, s1, t1, outb,
     u2a, u2b, u2c, u2d, r2c, f2, s2, t2,
     u3a, u3b, u3c, r3c, f3, s3, t3,
-    onehot, wrow, swap, swapped, comb, zrows, table,
+    onehot, wrow, swap, swapped, comb, zrows, table, partner, weight,
     load_sem, a_send, a_recv, b_send, b_recv, g_send, g_recv, out_sem,
 ):
     row = lax.axis_index("row")
@@ -132,15 +132,20 @@
         loads.append((sigma.at[0, :, cols], s1.at[t, own, :]))
         loads.append((state.at[0, :, :, cols], u1a.at[:, t, own, :]))
         loads.append((forcing.at[0, :, :, cols], f1.at[:, t, own, :]))
+    loads = [(partner_in, partner), (weight_in, weight)] + loads
     loads = [pltpu.make_async_copy(src, dst, load_sem.at[i]) for i, (src, dst) in enumerate(loads)]
     for copy in loads:
         copy.start()
+    for copy in loads[:2]:
+        copy.wait()
 
     lane = lanes()
     pick = pair_pick()
     low = lane % 8
     for k in range(4):
-        slot = lax.rem(partner[0, pl.ds(8 * k, 8), :], 8)
+        slot = jnp.zeros((8, 128), jnp.int32)
+        for i in range(8):
+            slot = jnp.where(rows_of() == i, partner[0, 0, 8 * k + i] & 7, slot)
         onehot[pl.ds(O1 + 8 * k, 8), :] = (slot == low).astype(jnp.float32)
     weights = jnp.zeros((8, 128), jnp.float32)
     for d, block in enumerate((left, b, right)):
@@ -148,7 +153,7 @@
             weights = jnp.where((rows_of() == d) & (low == p), weight[0, p * NB + block], weights)
     wrow[...] = weights
 
-    for copy in loads:
+    for copy in loads[2:]:
         copy.wait()
     for k in range(2):
         r = O2 + 8 * k
@@ -378,7 +383,9 @@
     scale8 = jnp.zeros((8, 8), jnp.float32)
     for k in range(8):
         scale8 = jnp.where(lanes((8, 8)) == k, weight[0, 8 * b + k], scale8)
-    loop_out[0] = (cells * scale8)[0:V]
+    cells = cells * scale8
+    for v in range(V):
+        loop_out[v] = cells[v : v + 1]
 
     rotate = (lane & ~7) | ((lane + (near_other >> 7)) & 7)
     corr = jnp.where(
@@ -430,25 +437,27 @@
     buffers += [middle] * 6 + [(2, R2, 128)] * 2
     buffers += [coarse] * 5 + [(1, R3, 128)] * 2
     buffers += [(R1, 128), (8, 128), (8, 128), (8, 128), (8, 128), (NZ, 128), (NX * NY, NZ, 128)]
-    any_space = pl.BlockSpec(memory_space=pl.ANY)
-    smem = pl.BlockSpec(memory_space=pltpu.SMEM)
+    hbm = pl.BlockSpec(memory_space=pltpu.HBM)
     vmem = pl.BlockSpec(memory_space=pltpu.VMEM)
     dma = pltpu.SemaphoreType.DMA
-    return pl.pallas_call(
+    placed = (state, forcing, sigma, partner.reshape(1, 1, 32), loop_weight)
+    solved, corrected = pl.pallas_call(
         kernel,
         out_shape=(
-            jax.ShapeDtypeStruct((1, V, 32, 512), f32),
-            jax.ShapeDtypeStruct((1, V, 8), f32),
+            pltpu.VMEM((1, V, 32, 512), f32),
+            pltpu.VMEM((V, 1, 8), f32),
         ),
-        in_specs=[any_space, any_space, any_space, vmem, smem, smem],
-        out_specs=(any_space, vmem),
+        in_specs=[hbm] * 5 + [pl.BlockSpec(memory_space=pltpu.SMEM)],
+        out_specs=(vmem, vmem),
         scratch_shapes=[pltpu.VMEM(shape, f32) for shape in buffers]
-        + [dma((12,)), dma((8,)), dma((8,)), dma((6,)), dma((6,)), dma((3,)), dma((3,)), dma((4,))],
+        + [pltpu.SMEM((1, 1, 32), jnp.int32), pltpu.SMEM((1, 1024), f32)]
+        + [dma((15,)), dma((8,)), dma((8,)), dma((6,)), dma((6,)), dma((3,)), dma((3,)), dma((4,))],
         compiler_params=pltpu.CompilerParams(
             collective_id=0, has_side_effects=True, vmem_limit_bytes=40 * 1024 * 1024
         ),
         name="fas_cycle",
-    )(state, forcing, sigma, partner, loop_weight, offset)
+    )(*[pltpu.with_memory_space_constraint(x, pltpu.HBM) for x in placed], offset)
+    return solved, corrected.reshape(1, V, 8)
 
 
 def solution(mesh):

time: 41.1 us -> 35.6 us (0.87)
  local copies, waits for them, and re-layouts: 4.77 us -> 1.3 us
  Pallas kernels: 34.3 us -> 32.3 us
    unnamed x12 -> x2, local copies, waits for them, and re-layouts: 4.19 us -> 1.3 us
    pallas_call x1, Pallas kernels: 34.3 us -> 32.3 us  [body(): pl.pallas_call(kernel, out_shape=(pltpu.VMEM((1, V, 32, 512), f32), pltpu...]
    pallas_call x1 -> x0, local copies, waits for them, and re-layouts: 0.58 us -> none  [body(): pl.pallas_call(kernel, out_shape=(jax.ShapeDtypeStruct((1, V, 32, 512), f...]
where the time goes in v2:
time: 35.6 us; the launch traced here: 34.9 us
  Pallas kernels  32.3 us (91%)
  local copies, waits for them, and re-layouts  1.3 us (4%)
  between operations  1.29 us (4%)
    pallas_call x1, Pallas kernels, body(): pl.pallas_call(kernel, out_shape=(pltpu.VMEM((1, V, 32, 512), f32), pltpu...  32.3 us
    unnamed x2, local copies, waits for them, and re-layouts  1.3 us

profile of v2, /device:TPU:0, one launch (start us, length us, event | category | flops | bytes accessed | tf_op | source)
XLA Modules:
  0.0 34.9 jit_solution(16287837153630223369)
XLA Ops:
  1.3 32.3 %fas_cycle.1 = (f32[1,5,32,512]{3,2,1,0:T(8,128)S(1)}, f32[5,1,8]{2,1,0:T(1,128)S(1)}) custom-call(f32[1,5,32,512]{3,2,1,0:T(8,128)} %state.1, f32[1,5,32,512]{3,2,1,0:T(8,128)} %forcing.1, f32[1,32,512]{2,1,0:T(8,128)} %sigma.1, s32[1,1,32]{2,1,0:T(1,128)} %bitcast.3, f32[1,1024]{1,0:T(1,128)} %weight_in.1, s32[1]{0:T(128)S(6)} %copy.12.offset), custom_call_target="tpu_custom_call" | custom-call | tf_op jit(solution)/shard_map/fas_cycle/pallas_call | solution.py:444
  33.6 0.7 %copy.10 = f32[1,5,32,512]{3,2,1,0:T(8,128)} copy(f32[1,5,32,512]{3,2,1,0:T(8,128)S(1)} %get-tuple-element.6) | data formatting | bytes 655360
  34.3 0.6 %copy.11 = f32[1,5,8]{2,0,1:T(1,128)} copy(f32[1,5,8]{2,0,1:T(1,128)S(1)} %bitcast.2) | data formatting | bytes 320

commit v3 on v2

--- a/solution.py
+++ b/solution.py
@@ -16,6 +16,17 @@
 
 
 def loop(first, tiles, body):
+    if isinstance(first, tuple):
+        low, second, third, high = first
+
+        def strips(k, carry):
+            body(low + k * (second - low))
+            body(third + k * (high - third))
+            return carry
+
+        lax.fori_loop(0, 2, strips, 0)
+        return
+
     def step(k, carry):
         body(first + 8 * k)
         return carry
@@ -59,14 +70,14 @@
     return centre, out
 
 
-def section(dst, start, src, f_ref, s_ref, tau_ref, first, tiles, nt, scale, portion, shift=0):
+def section(dst, start, src, f_ref, s_ref, tau_ref, first, tiles, nt, scale, portion):
     def body(r):
         here = pl.ds(r, 8)
         _, out = apply_l(src, s_ref, r, nt, scale)
         for t in range(nt):
             tau = tau_ref[t, here, :] * portion
             for v in range(V):
-                dst[v, t, pl.ds(r - shift, 8), :] = start[v, t, here, :] + tau * (
+                dst[v, t, here, :] = start[v, t, here, :] + tau * (
                     f_ref[v, t, here, :] - out[v][t]
                 )
 
@@ -101,11 +112,11 @@
 
 def kernel(
     state, forcing, sigma, partner_in, weight_in, offset, out, loop_out,
-    u1a, u1b, u1c, u1d, f1, s1, t1, outb,
+    u1a, u1b, u1c, u1d, u1e, f1, s1, t1,
     u2a, u2b, u2c, u2d, r2c, f2, s2, t2,
     u3a, u3b, u3c, r3c, f3, s3, t3,
     onehot, wrow, swap, swapped, comb, zrows, table, partner, weight,
-    load_sem, a_send, a_recv, b_send, b_recv, g_send, g_recv, out_sem,
+    load_sem, a_send, a_recv, b_send, b_recv, g_send, g_recv,
 ):
     row = lax.axis_index("row")
     b = lax.axis_index("blk")
@@ -185,13 +196,18 @@
     a_copies = fine(u1a, 2, 6, 0) + fine(f1, 2, 5, 2) + fine(s1, 1, 5, 4)
     a_late = fine(onehot, 0, 4, 6)
     b_early = across(s2, 1, *wide, b_send, b_recv, 0)
+    step_size(t1, s1, O1, 4, 4, 1.0)
+    section(u1b, u1a, u1a, f1, s1, t1, O1 + 4, 3, 4, 1.0, 1.0 / 3.0)
+    section(u1c, u1a, u1b, f1, s1, t1, O1 + 8, 2, 4, 1.0, 0.5)
+    section(u1e, u1a, u1c, f1, s1, t1, O1 + 12, 1, 4, 1.0, 1.0)
     for copy in a_copies:
         copy.wait_recv()
-
-    step_size(t1, s1, O1 - 8, 6, 4, 1.0)
-    section(u1b, u1a, u1a, f1, s1, t1, O1 - 8, 6, 4, 1.0, 1.0 / 3.0)
-    section(u1c, u1a, u1b, f1, s1, t1, O1 - 4, 5, 4, 1.0, 0.5)
-    section(u1b, u1a, u1c, f1, s1, t1, O1 - 4, 5, 4, 1.0, 1.0)
+    step_size(t1, s1, O1 - 8, 1, 4, 1.0)
+    step_size(t1, s1, O1 + 32, 1, 4, 1.0)
+    strips = dict(f_ref=f1, s_ref=s1, tau_ref=t1, nt=4, scale=1.0)
+    section(u1b, u1a, u1a, first=(O1 - 8, O1 - 4, O1 + 28, O1 + 32), tiles=4, portion=1.0 / 3.0, **strips)
+    section(u1c, u1a, u1b, first=(O1 - 4, O1, O1 + 24, O1 + 28), tiles=4, portion=0.5, **strips)
+    section(u1e, u1a, u1c, first=(O1 - 4, O1 + 4, O1 + 20, O1 + 28), tiles=4, portion=1.0, **strips)
 
     target = jnp.where(row == 0, 127, 0)
     at_target = jnp.zeros((8, 128), jnp.int32) + target
@@ -201,7 +217,7 @@
 
     def residual(r):
         here = pl.ds(r, 8)
-        _, out_l = apply_l(u1b, s1, r, 4, 1.0)
+        _, out_l = apply_l(u1e, s1, r, 4, 1.0)
         mixed = jnp.zeros((8, 128), jnp.float32)
         for v in range(V):
             rest = [f1[v, t, here, :] - out_l[v][t] for t in range(4)]
@@ -222,7 +238,7 @@
 
     for k, r in enumerate((-1, 7, 9)):
         for v in range(V):
-            tiles = coarsen_rows(lambda t, rows, v=v: u1b[v, t, rows, :], O1 + 2 * r, 4, pick)
+            tiles = coarsen_rows(lambda t, rows, v=v: u1e[v, t, rows, :], O1 + 2 * r, 4, pick)
             for t in range(2):
                 u2a[v, t, pl.ds(O2 + r, 8), :] = tiles[t]
     for r in (0, 8):
@@ -268,9 +284,15 @@
         recv_sem=g_recv.at[2], device_id=xy_peers[0], device_id_type=MESH,
     )
 
-    for copy in b_early + b_copies:
+    for copy in b_early:
         copy.wait_recv()
     step_size(t2, s2, O2 - 16, 6, 2, 0.25)
+    for k in range(3):
+        here = pl.ds(O3 - 8 + 8 * k, 8)
+        s3[0, here, :] = coarsen_rows(lambda t, rows: s2[t, rows, :], O2 - 16 + 16 * k, 2, pick)[0]
+        t3[0, here, :] = 0.8 / (s3[0, here, :] + 1.75)
+    for copy in b_copies:
+        copy.wait_recv()
     portion = 1.0 / 3.0
 
     def middle_first(r):
@@ -299,8 +321,6 @@
     for k in range(3):
         r, f = O3 - 8 + 8 * k, O2 - 16 + 16 * k
         here = pl.ds(r, 8)
-        s3[0, here, :] = coarsen_rows(lambda t, rows: s2[t, rows, :], f, 2, pick)[0]
-        t3[0, here, :] = 0.8 / (s3[0, here, :] + 1.75)
         for v in range(V):
             u3a[v, 0, here, :] = coarsen_rows(lambda t, rows, v=v: u2b[v, t, rows, :], f, 2, pick)[0]
             r3c[v, 0, here, :] = coarsen_rows(lambda t, rows, v=v: u2c[v, t, rows, :], f, 2, pick)[0]
@@ -345,7 +365,7 @@
                     more = jnp.take_along_axis(gain, spread[part], axis=1)
                     for odd in range(2):
                         rows = pl.ds(f + odd, 8, stride=2)
-                        u1d[v, t, rows, :] = u1b[v, t, rows, :] + more
+                        u1d[v, t, rows, :] = u1e[v, t, rows, :] + more
 
     for copy in a_late:
         copy.wait_recv()
@@ -414,26 +434,39 @@
 
     section(u1c, u1d, u1d, f1, s1, t1, O1 - 4, 5, 4, 1.0, 1.0 / 3.0)
     section(u1b, u1d, u1c, f1, s1, t1, O1 - 4, 5, 4, 1.0, 0.5)
-    section(outb, u1d, u1b, f1, s1, t1, O1, 4, 4, 1.0, 1.0, shift=O1)
-
-    stores = [
-        pltpu.make_async_copy(outb.at[:, t], out.at[0, :, :, pl.ds(t * 128, 128)], out_sem.at[t])
-        for t in range(4)
-    ]
-    for copy in stores:
-        copy.start()
+
+    def last(r):
+        here = pl.ds(r, 8)
+        _, out_l = apply_l(u1b, s1, r, 4, 1.0)
+        for t in range(4):
+            tau = t1[t, here, :]
+            for v in range(V):
+                out[0, v, pl.ds(r - O1, 8), 128 * t : 128 * t + 128] = u1d[v, t, here, :] + tau * (
+                    f1[v, t, here, :] - out_l[v][t]
+                )
+
+    loop(O1, 4, last)
     for copy in a_copies + a_late + b_early + b_copies + [to_core]:
         copy.wait_send()
     z_all.wait_send()
     t_all.wait_send()
-    for copy in stores:
+
+
+def write_out(solved, corrected, out, loop_out, sem):
+    copies = [
+        pltpu.make_async_copy(solved, out, sem.at[0]),
+        pltpu.make_async_copy(corrected, loop_out, sem.at[1]),
+    ]
+    for copy in copies:
+        copy.start()
+    for copy in copies:
         copy.wait()
 
 
 def body(state, forcing, sigma, partner, loop_weight, offset):
     f32 = jnp.float32
     fine, middle, coarse = (V, 4, R1, 128), (V, 2, R2, 128), (V, 1, R3, 128)
-    buffers = [fine] * 5 + [(4, R1, 128)] * 2 + [(V, 4, 32, 128)]
+    buffers = [fine] * 6 + [(4, R1, 128)] * 2
     buffers += [middle] * 6 + [(2, R2, 128)] * 2
     buffers += [coarse] * 5 + [(1, R3, 128)] * 2
     buffers += [(R1, 128), (8, 128), (8, 128), (8, 128), (8, 128), (NZ, 128), (NX * NY, NZ, 128)]
@@ -451,12 +484,26 @@
         out_specs=(vmem, vmem),
         scratch_shapes=[pltpu.VMEM(shape, f32) for shape in buffers]
         + [pltpu.SMEM((1, 1, 32), jnp.int32), pltpu.SMEM((1, 1024), f32)]
-        + [dma((15,)), dma((8,)), dma((8,)), dma((6,)), dma((6,)), dma((3,)), dma((3,)), dma((4,))],
+        + [dma((15,)), dma((8,)), dma((8,)), dma((6,)), dma((6,)), dma((3,)), dma((3,))],
         compiler_params=pltpu.CompilerParams(
             collective_id=0, has_side_effects=True, vmem_limit_bytes=40 * 1024 * 1024
         ),
         name="fas_cycle",
     )(*[pltpu.with_memory_space_constraint(x, pltpu.HBM) for x in placed], offset)
+    solved = pltpu.with_memory_space_constraint(solved, pltpu.VMEM)
+    corrected = pltpu.with_memory_space_constraint(corrected, pltpu.VMEM)
+    solved, corrected = pl.pallas_call(
+        write_out,
+        out_shape=(
+            jax.ShapeDtypeStruct((1, V, 32, 512), f32),
+            jax.ShapeDtypeStruct((V, 1, 8), f32),
+        ),
+        in_specs=[vmem] * 2,
+        out_specs=(pl.BlockSpec(memory_space=pl.ANY),) * 2,
+        scratch_shapes=[dma((2,))],
+        compiler_params=pltpu.CompilerParams(vmem_limit_bytes=40 * 1024 * 1024),
+        name="write_out",
+    )(solved, corrected)
     return solved, corrected.reshape(1, V, 8)
 
 

time: 35.6 us -> 34.2 us (0.961)
  local copies, waits for them, and re-layouts: 1.3 us -> 0 us
    unnamed x2 -> x0, local copies, waits for them, and re-layouts: 1.3 us -> none
    pallas_call x1, Pallas kernels: 32.3 us -> 31.5 us  [body(): pl.pallas_call(kernel, out_shape=(pltpu.VMEM((1, V, 32, 512), f32), pltpu...]
    pallas_call x0 -> x1, Pallas kernels: none -> 0.75 us  [body(): pl.pallas_call(write_out, out_shape=(jax.ShapeDtypeStruct((1, V, 32, 512)...]
where the time goes in v3:
time: 34.2 us; the launch traced here: 33.5 us
  Pallas kernels  32.2 us (94%)
  between operations  1.29 us (4%)
    pallas_call x1, Pallas kernels, body(): pl.pallas_call(kernel, out_shape=(pltpu.VMEM((1, V, 32, 512), f32), pltpu...  31.5 us
    pallas_call x1, Pallas kernels, body(): pl.pallas_call(write_out, out_shape=(jax.ShapeDtypeStruct((1, V, 32, 512)...  0.75 us

profile of v3, /device:TPU:0, one launch (start us, length us, event | category | flops | bytes accessed | tf_op | source)
XLA Modules:
  0.0 33.5 jit_solution(8141469616034800488)
XLA Ops:
  1.3 31.5 %fas_cycle.1 = (f32[1,5,32,512]{3,2,1,0:T(8,128)S(1)}, f32[5,1,8]{2,1,0:T(1,128)S(1)}) custom-call(f32[1,5,32,512]{3,2,1,0:T(8,128)} %state.1, f32[1,5,32,512]{3,2,1,0:T(8,128)} %forcing.1, f32[1,32,512]{2,1,0:T(8,128)} %sigma.1, s32[1,1,32]{2,1,0:T(1,128)} %bitcast.2, f32[1,1024]{1,0:T(1,128)} %weight_in.1, s32[1]{0:T(128)S(6)} %copy.8.offset), custom_call_target="tpu_custom_call" | custom-call | tf_op jit(solution)/shard_map/fas_cycle/pallas_call | solution.py:477
  32.8 0.7 %write_out.1 = (f32[1,5,32,512]{3,2,1,0:T(8,128)}, f32[5,1,8]{2,1,0:T(1,128)}) custom-call(f32[1,5,32,512]{3,2,1,0:T(8,128)S(1)} %get-tuple-element.6.solved, f32[5,1,8]{2,1,0:T(1,128)S(1)} %get-tuple-element.7.corrected), custom_call_target="tpu_custom_call" | custom-call | tf_op jit(solution)/shard_map/write_out/pallas_call | solution.py:495

commit v4 on v3

--- a/solution.py
+++ b/solution.py
@@ -31,7 +31,7 @@
         body(first + 8 * k)
         return carry
 
-    lax.fori_loop(0, tiles, step, 0, unroll=2 if tiles % 2 == 0 else 1)
+    lax.fori_loop(0, tiles, step, 0, unroll=2 if tiles == 4 else 3 if tiles == 6 else tiles)
 
 
 def lanes(shape=(8, 128)):
@@ -209,6 +209,14 @@
     section(u1c, u1a, u1b, first=(O1 - 4, O1, O1 + 24, O1 + 28), tiles=4, portion=0.5, **strips)
     section(u1e, u1a, u1c, first=(O1 - 4, O1 + 4, O1 + 20, O1 + 28), tiles=4, portion=1.0, **strips)
 
+    for k, r in enumerate((-1, 7, 9)):
+        for v in range(V):
+            tiles = coarsen_rows(lambda t, rows, v=v: u1e[v, t, rows, :], O1 + 2 * r, 4, pick)
+            for t in range(2):
+                u2a[v, t, pl.ds(O2 + r, 8), :] = tiles[t]
+    b_copies = across(
+        u2a, 2, ((O2 - 1, 16), (O2 + 1, 16)), ((O2 - 17, 16), (O2 + 17, 16)), b_send, b_recv, 2
+    )
     target = jnp.where(row == 0, 127, 0)
     at_target = jnp.zeros((8, 128), jnp.int32) + target
     variable = (lane - 64 * row) // 8
@@ -236,19 +244,11 @@
     )
     to_core.start()
 
-    for k, r in enumerate((-1, 7, 9)):
-        for v in range(V):
-            tiles = coarsen_rows(lambda t, rows, v=v: u1e[v, t, rows, :], O1 + 2 * r, 4, pick)
-            for t in range(2):
-                u2a[v, t, pl.ds(O2 + r, 8), :] = tiles[t]
     for r in (0, 8):
         for v in range(V):
             tiles = coarsen_rows(lambda t, rows, v=v: u1c[v, t, rows, :], O1 + 2 * r, 4, pick)
             for t in range(2):
                 r2c[v, t, pl.ds(O2 + r, 8), :] = tiles[t]
-    b_copies = across(
-        u2a, 2, ((O2 - 1, 16), (O2 + 1, 16)), ((O2 - 17, 16), (O2 + 17, 16)), b_send, b_recv, 2
-    )
     b_copies += across(r2c, 2, *wide, b_send, b_recv, 4)
 
     to_core.wait_recv()

time: 34.2 us -> 32.6 us (0.953)
  Pallas kernels: 32.2 us -> 30.9 us
    pallas_call x1, Pallas kernels: 31.5 us -> 30.2 us  [body(): pl.pallas_call(kernel, out_shape=(pltpu.VMEM((1, V, 32, 512), f32), pltpu...]
where the time goes in v4:
time: 32.6 us; the launch traced here: 32.2 us
  Pallas kernels  30.9 us (95%)
  between operations  1.29 us (4%)
    pallas_call x1, Pallas kernels, body(): pl.pallas_call(kernel, out_shape=(pltpu.VMEM((1, V, 32, 512), f32), pltpu...  30.2 us
    pallas_call x1, Pallas kernels, body(): pl.pallas_call(write_out, out_shape=(jax.ShapeDtypeStruct((1, V, 32, 512)...  0.75 us

profile of v4, /device:TPU:0, one launch (start us, length us, event | category | flops | bytes accessed | tf_op | source)
XLA Modules:
  0.0 32.2 jit_solution(17514738212432599804)
XLA Ops:
  1.3 30.2 %fas_cycle.1 = (f32[1,5,32,512]{3,2,1,0:T(8,128)S(1)}, f32[5,1,8]{2,1,0:T(1,128)S(1)}) custom-call(f32[1,5,32,512]{3,2,1,0:T(8,128)} %state.1, f32[1,5,32,512]{3,2,1,0:T(8,128)} %forcing.1, f32[1,32,512]{2,1,0:T(8,128)} %sigma.1, s32[1,1,32]{2,1,0:T(1,128)} %bitcast.2, f32[1,1024]{1,0:T(1,128)} %weight_in.1, s32[1]{0:T(128)S(6)} %copy.8.offset), custom_call_target="tpu_custom_call" | custom-call | tf_op jit(solution)/shard_map/fas_cycle/pallas_call | solution.py:477
  31.5 0.7 %write_out.1 = (f32[1,5,32,512]{3,2,1,0:T(8,128)}, f32[5,1,8]{2,1,0:T(1,128)}) custom-call(f32[1,5,32,512]{3,2,1,0:T(8,128)S(1)} %get-tuple-element.6.solved, f32[5,1,8]{2,1,0:T(1,128)S(1)} %get-tuple-element.7.corrected), custom_call_target="tpu_custom_call" | custom-call | tf_op jit(solution)/shard_map/write_out/pallas_call | solution.py:495

commit v5 on v4

--- a/solution.py
+++ b/solution.py
@@ -284,6 +284,26 @@
         recv_sem=g_recv.at[2], device_id=xy_peers[0], device_id_type=MESH,
     )
 
+    turn = jnp.where(row == 0, offset[0], 1024 - offset[0])
+    index = rows_of()
+    cell_own = 8 * b + index
+    near_own = lax.rem(b + NB - 1 + index, NB)
+    cell_other = (cell_own + turn) & 1023
+    near_other = (near_own + turn) & 1023
+
+    def chosen(block):
+        block = block & 127
+        place = ((block >> 5) * 4 + (block & 3)) * 8 + ((block >> 2) & 7)
+        return (place == lane).astype(jnp.float32)
+
+    wanted = jnp.concatenate(
+        [chosen(cell_own), chosen(near_own), chosen(cell_other), chosen(near_other)], axis=0
+    )
+    scale8 = jnp.zeros((8, 8), jnp.float32)
+    for k in range(8):
+        scale8 = jnp.where(lanes((8, 8)) == k, weight[0, 8 * b + k], scale8)
+    rotate = (lane & ~7) | ((lane + (near_other >> 7)) & 7)
+    summed = (index == lane // 8).astype(jnp.float32)
     for copy in b_early:
         copy.wait_recv()
     step_size(t2, s2, O2 - 16, 6, 2, 0.25)
@@ -291,19 +311,29 @@
         here = pl.ds(O3 - 8 + 8 * k, 8)
         s3[0, here, :] = coarsen_rows(lambda t, rows: s2[t, rows, :], O2 - 16 + 16 * k, 2, pick)[0]
         t3[0, here, :] = 0.8 / (s3[0, here, :] + 1.75)
-    for copy in b_copies:
+    for copy in b_copies[0:2]:
+        copy.wait_recv()
+
+    def middle_l(r):
+        here = pl.ds(r, 8)
+        _, out_l = apply_l(u2a, s2, r, 2, 0.25)
+        for t in range(2):
+            for v in range(V):
+                f2[v, t, here, :] = out_l[v][t]
+
+    loop(O2 - 16, 6, middle_l)
+    for copy in b_copies[2:4]:
         copy.wait_recv()
     portion = 1.0 / 3.0
 
     def middle_first(r):
         here = pl.ds(r, 8)
-        centre, out_l = apply_l(u2a, s2, r, 2, 0.25)
         for t in range(2):
             tau = t2[t, here, :] * portion
             for v in range(V):
                 rest = r2c[v, t, here, :]
-                f2[v, t, here, :] = out_l[v][t] + rest
-                u2b[v, t, here, :] = centre[v][t] + tau * rest
+                f2[v, t, here, :] += rest
+                u2b[v, t, here, :] = u2a[v, t, here, :] + tau * rest
 
     loop(O2 - 16, 6, middle_first)
     section(u2c, u2a, u2b, f2, s2, t2, O2 - 16, 6, 2, 0.25, 0.5)
@@ -371,21 +401,6 @@
         copy.wait_recv()
     t_all.wait_recv()
 
-    turn = jnp.where(row == 0, offset[0], 1024 - offset[0])
-    index = rows_of()
-    cell_own = 8 * b + index
-    near_own = lax.rem(b + NB - 1 + index, NB)
-    cell_other = (cell_own + turn) & 1023
-    near_other = (near_own + turn) & 1023
-
-    def chosen(block):
-        block = block & 127
-        place = ((block >> 5) * 4 + (block & 3)) * 8 + ((block >> 2) & 7)
-        return (place == lane).astype(jnp.float32)
-
-    wanted = jnp.concatenate(
-        [chosen(cell_own), chosen(near_own), chosen(cell_other), chosen(near_other)], axis=0
-    )
     found = jnp.dot(
         wanted, table[...].reshape(NB, 128), precision=HIGH, preferred_element_type=jnp.float32
     )
@@ -396,18 +411,13 @@
     picked = jnp.where(valid & (low == (b // 16)), own[0:8], 0.0) + jnp.where(
         valid & (low == (cell_other >> 7)), other[0:8], 0.0
     )
-    summed = (index == lane // 8).astype(jnp.float32)
     cells = lax.dot_general(
         summed, picked, (((1,), (1,)), ((), ())), precision=HIGH, preferred_element_type=jnp.float32
     )
-    scale8 = jnp.zeros((8, 8), jnp.float32)
-    for k in range(8):
-        scale8 = jnp.where(lanes((8, 8)) == k, weight[0, 8 * b + k], scale8)
     cells = cells * scale8
     for v in range(V):
         loop_out[v] = cells[v : v + 1]
 
-    rotate = (lane & ~7) | ((lane + (near_other >> 7)) & 7)
     corr = jnp.where(
         valid, wrow[...] * (own[8:16] + jnp.take_along_axis(other[8:16], rotate, axis=1)), 0.0
     )

time: 32.6 us -> 32.4 us (level)
  no operation moved by 1% of the time
where the time goes in v5:
time: 32.4 us; the launch traced here: 32 us
  Pallas kernels  30.8 us (95%)
  between operations  1.29 us (4%)
    pallas_call x1, Pallas kernels, body(): pl.pallas_call(kernel, out_shape=(pltpu.VMEM((1, V, 32, 512), f32), pltpu...  30 us
    pallas_call x1, Pallas kernels, body(): pl.pallas_call(write_out, out_shape=(jax.ShapeDtypeStruct((1, V, 32, 512)...  0.75 us

profile of v5, /device:TPU:0, one launch (start us, length us, event | category | flops | bytes accessed | tf_op | source)
XLA Modules:
  0.0 32.0 jit_solution(18357275693031185707)
XLA Ops:
  1.3 30.0 %fas_cycle.1 = (f32[1,5,32,512]{3,2,1,0:T(8,128)S(1)}, f32[5,1,8]{2,1,0:T(1,128)S(1)}) custom-call(f32[1,5,32,512]{3,2,1,0:T(8,128)} %state.1, f32[1,5,32,512]{3,2,1,0:T(8,128)} %forcing.1, f32[1,32,512]{2,1,0:T(8,128)} %sigma.1, s32[1,1,32]{2,1,0:T(1,128)} %bitcast.2, f32[1,1024]{1,0:T(1,128)} %weight_in.1, s32[1]{0:T(128)S(6)} %copy.8.offset), custom_call_target="tpu_custom_call" | custom-call | tf_op jit(solution)/shard_map/fas_cycle/pallas_call | solution.py:487
  31.3 0.7 %write_out.1 = (f32[1,5,32,512]{3,2,1,0:T(8,128)}, f32[5,1,8]{2,1,0:T(1,128)}) custom-call(f32[1,5,32,512]{3,2,1,0:T(8,128)S(1)} %get-tuple-element.6.solved, f32[5,1,8]{2,1,0:T(1,128)S(1)} %get-tuple-element.7.corrected), custom_call_target="tpu_custom_call" | custom-call | tf_op jit(solution)/shard_map/write_out/pallas_call | solution.py:505
